TPU v7x, 32 devices: a whole 2x2x4 slice. The times are simulated.
32 devices in a mesh: groups: 2 (over x), node: 16 (over z, y, core).
Axes of the slice: x: 2, y: 2, z: 4, core: 2. Of those that a mesh axis runs over, the one named last changes fastest.
Arguments:
- tokens: bfloat16 [4096, 4096], P(('groups', 'node')), parts along dimension 0, may hold values from -6 to 6
- steer_table: bfloat16 [256, 4096], P(('groups', 'node')), parts along dimension 0, may hold values from -6 to 6
- steer_index: int32 [4096], P(('groups', 'node')), parts along dimension 0, may hold values from 0 to 127
- sweep_coef: float32 [4096], P(('groups', 'node')), parts along dimension 0, may hold values from -3 to 3
- expert_ids: int32 [4096, 4], P(('groups', 'node')), parts along dimension 0, may hold values from 0 to 7, all different within a row; in each aligned block of 128 rows (0 to 127, 128 to 255, ...) at most 80 rows name the same one
- gate_level: int32 [4096, 4], P(('groups', 'node')), parts along dimension 0, may hold values from 0 to 15
- w_gate: bfloat16 [16, 4096, 768], P('node'), may hold values from -0.09375 to 0.09375
- w_up: bfloat16 [16, 4096, 768], P('node'), may hold values from -0.09375 to 0.09375
- w_down: bfloat16 [16, 768, 4096], P('node'), may hold values from -0.15625 to 0.15625
Outputs:
- mixed: bfloat16 [4096, 4096], P(('groups', 'node')), parts along dimension 0
There are 2 independent parts, one for each index of `groups`. A program takes and returns all parts, laid end to end along the dimension named above; an argument that names none is the same for every part. Nothing has to cross between parts.
Inputs may be any that keep to these rules, and one draw needn't show every extreme that they name: `expert_ids`: each row names 4 different experts. Among the rows of one device no expert is named more than 80 times, a bound that some block reaches.
All inputs are finite; a program needn't handle non-finite values.
Results may differ from a plain program's by a relative error of at most 0.0085.
Values may be sent and summed in bfloat16 or wider, within the bound.
A program may use at most 128 MiB of HBM per device.

v0:
```python
import jax
import jax.numpy as jnp
from jax import lax
from jax.sharding import PartitionSpec as P


def on_device(
    tokens, steer_table, steer_index, sweep_coef, expert_ids, gate_level, w_gate, w_up, w_down
):
    tok_rows, width = tokens.shape
    top_count = expert_ids.shape[1]
    nodes = lax.axis_size("node")
    experts = nodes // 2
    slots = 2 * ((tok_rows * top_count * 5 + 8 * experts - 1) // (8 * experts))
    piece = lax.all_gather(steer_table, "node", axis=0, tiled=True)
    columns = lax.iota(jnp.int32, piece.shape[0])
    picker = (steer_index[:, None] == columns[None, :]).astype(jnp.bfloat16)
    steer = jnp.dot(picker, piece, preferred_element_type=jnp.float32)
    steered = tokens.astype(jnp.float32) + sweep_coef[:, None] * steer
    scale = lax.rsqrt(jnp.mean(steered * steered, axis=1, keepdims=True) + 1e-06)
    normed = (steered * scale).astype(jnp.bfloat16)
    flat_ids = expert_ids.reshape(-1)
    onehot = (flat_ids[:, None] == lax.iota(jnp.int32, experts)[None, :]).astype(jnp.int32)
    rank = jnp.cumsum(onehot, axis=0) - onehot
    slot_of = jnp.sum(onehot * rank, axis=1)
    target = (flat_ids * slots + slot_of).reshape(tok_rows, top_count)
    places = lax.iota(jnp.int32, experts * slots)
    matched = target[:, :, None] == places[None, None, :]
    select = jnp.any(matched, axis=1).astype(jnp.bfloat16)
    levels = (gate_level + 1).astype(jnp.float32)
    share = levels / jnp.sum(levels, axis=1, keepdims=True)
    mixing = jnp.sum(jnp.where(matched, share[:, :, None], 0.0), axis=1)
    packed = jnp.einsum("tr,td->rd", select, normed, preferred_element_type=jnp.float32).astype(
        jnp.bfloat16
    )
    doubled = jnp.broadcast_to(packed.reshape(experts, 1, slots, width), (experts, 2, slots, width))
    doubled = doubled.reshape(nodes, slots, width)
    block = lax.all_to_all(doubled, "node", split_axis=0, concat_axis=0, tiled=True)
    rows = block.reshape(-1, width)
    gate = jnp.dot(rows, w_gate[0], preferred_element_type=jnp.float32)
    upper = jnp.dot(rows, w_up[0], preferred_element_type=jnp.float32)
    act = (jax.nn.silu(gate) * upper).astype(jnp.bfloat16)
    partial_value = (
        jnp.dot(act, w_down[0], preferred_element_type=jnp.float32)
        .astype(jnp.bfloat16)
        .reshape(block.shape)
    )
    back = lax.all_to_all(partial_value, "node", split_axis=0, concat_axis=0, tiled=True).reshape(
        experts, 2, slots, width
    )
    summed = back[:, 0].astype(jnp.float32) + back[:, 1].astype(jnp.float32)
    total = summed.astype(jnp.bfloat16).reshape(experts * slots, width)
    mix_high = mixing.astype(jnp.bfloat16)
    mix_low = (mixing - mix_high.astype(jnp.float32)).astype(jnp.bfloat16)
    mixed = jnp.dot(mix_high, total, preferred_element_type=jnp.float32)
    mixed = mixed + jnp.dot(mix_low, total, preferred_element_type=jnp.float32)
    return mixed.astype(jnp.bfloat16)


def solution(mesh):
    return jax.shard_map(
        on_device,
        mesh=mesh,
        in_specs=(
            P(("groups", "node"), None),
            P(("groups", "node"), None),
            P(("groups", "node")),
            P(("groups", "node")),
            P(("groups", "node"), None),
            P(("groups", "node"), None),
            P("node", None, None),
            P("node", None, None),
            P("node", None, None),
        ),
        out_specs=P(("groups", "node"), None),
        check_vma=False,
    )
```

profile of v0, /device:TPU:13, one launch (start us, length us, event | category | flops | bytes accessed | tf_op | source)
XLA Modules:
  0.0 576.2 jit_solution(3130127611829963497)
XLA Ops:
  6.5 0.7 all-gather.2.cloned.1.call-update
  7.3 0.8 copy.22
  8.0 0.1 eq.55
  8.2 0.1 eq.51
  8.3 1.1 reduce-window.6
  9.4 0.2 slice_reduce_fusion
  9.7 0.1 fusion.20
  9.8 0.1 reduce_sum.39
  10.0 0.7 multiply_add_fusion
  10.7 0.2 fusion.13
  10.9 36.9 %all-gather.2.cloned.1.call-done = bf16[128,4096]{1,0:T(8,128)(2,1)} async-done(((bf16[8,4096]{1,0:T(8,128)(2,1)}), bf16[128,4096]{1,0:T(8,128)(2,1)}) %all-gather.2.cloned.1.call-update) | async-done | bytes 1048592 | tf_op jit(solution)/shard_map/all_gather | solution.py:15
  47.8 2.2 multiply_reduce_fusion
  50.1 4.0 convolution_convert_fusion.1
  54.0 7.9 %broadcast_in_dim.30 = bf16[8,2,80,4096]{3,2,1,0:T(8,128)(2,1)} broadcast(bf16[8,80,4096]{2,1,0:T(8,128)(2,1)} %bitcast.37), dimensions={0,2,3} | broadcast | bytes 15728640 | tf_op jit(solution)/shard_map/broadcast_in_dim | solution.py:36
  62.0 233.0 %all_to_all.10 = bf16[16,80,4096]{2,1,0:T(8,128)(2,1)S(1)} all-to-all(bf16[16,80,4096]{2,1,0:T(8,128)(2,1)} %bitcast.36), channel_id=1, replica_groups=mesh['groups'=2,'node'=16] {'node'}, dimensions={0} | all-to-all | bytes 20971520 | tf_op jit(solution)/shard_map/all_to_all | solution.py:38
  295.0 11.8 %fusion.3 = f32[1280,768]{1,0:T(8,128)} fusion(bf16[1280,4096]{1,0:T(8,128)(2,1)S(1)} %bitcast.39, bf16[1,4096,768]{2,1,0:T(8,128)(2,1)} %param.15), kind=kOutput, calls=%fused_computation.6 | convolution fusion | flops 8053063680 | bytes 20709376 | tf_op jit(solution)/shard_map/dot_general | solution.py:40
  306.8 10.3 %fusion.10 = bf16[1280,768]{1,0:T(8,128)(2,1)S(1)} fusion(bf16[1280,4096]{1,0:T(8,128)(2,1)S(1)} %bitcast.40, bf16[1,4096,768]{2,1,0:T(8,128)(2,1)S(1)} %bitcast.42, f32[1280,768]{1,0:T(8,128)} %fusion.3), kind=kOutput, calls=%fused_computation.13 | convolution fusion | flops 8058961920 | bytes 22675456 | tf_op jit(solution)/shard_map/dot_general | solution.py:41
  317.1 10.6 %convolution_convert_fusion = bf16[1280,4096]{1,0:T(8,128)(2,1)} fusion(bf16[1280,768]{1,0:T(8,128)(2,1)S(1)} %fusion.10, bf16[1,768,4096]{2,1,0:T(8,128)(2,1)S(1)} %bitcast.44), kind=kOutput, calls=%fused_computation | convolution fusion | flops 8058306560 | bytes 18743296 | tf_op jit(solution)/shard_map/dot_general | solution.py:44
  327.7 5.3 all-to-all-start.1
  333.0 0.2 select_reduce_fusion
  333.3 227.0 %all-to-all-done.1 = bf16[16,80,4096]{2,1,0:T(8,128)(2,1)} async-done(((bf16[16,80,4096]{2,1,0:T(8,128)(2,1)}), bf16[16,80,4096]{2,1,0:T(8,128)(2,1)}, u32[]{:S(2)}, u32[]{:S(2)}) %all-to-all-start.1) | async-done | bytes 10485792 | tf_op jit(solution)/shard_map/all_to_all | solution.py:48
  560.3 6.1 %add_convert_fusion = bf16[8,1,80,4096]{3,2,1,0:T(8,128)(2,1)S(1)} fusion(bf16[8,2,80,4096]{3,2,1,0:T(8,128)(2,1)} %bitcast.9), kind=kLoop, calls=%fused_computation.1 | loop fusion | flops 10485760 | bytes 15728640 | tf_op jit(solution)/shard_map/convert_element_type | solution.py:52
  566.4 1.0 fusion.16
  567.4 2.0 fusion.6
  (20 shorter events, 0.2 us)
Async XLA Ops:
  6.5 41.3 %all-gather.2.cloned.1.call-start = ((), (), s32[]{:S(2)}) async-start(), calls=%async_computation.2 | async-start | bytes 1114112 | tf_op jit(solution)/shard_map/all_gather | solution.py:15
  62.0 244.8 %slice-start = ((s8[6291456]{0:T(1024)(128)(4,1)}), s8[4194304]{0:T(1024)(128)(4,1)S(1)}, s32[]{:S(2)}) async-start(s8[6291456]{0:T(1024)(128)(4,1)} %bitcast.41), calls=%async_computation.3 | async-start | bytes 8388608
  62.0 255.1 %slice-start.2 = ((s8[6291456]{0:T(1024)(128)(4,1)}), s8[4194304]{0:T(1024)(128)(4,1)S(1)}, s32[]{:S(2)}) async-start(s8[6291456]{0:T(1024)(128)(4,1)} %bitcast.43), calls=%async_computation.5 | async-start | bytes 8388608
  295.0 11.8 %slice-start.1 = ((s8[6291456]{0:T(1024)(128)(4,1)}), s8[2097152]{0:T(1024)(128)(4,1)S(1)}, s32[]{:S(2)}) async-start(s8[6291456]{0:T(1024)(128)(4,1)} %bitcast.41), calls=%async_computation.4 | async-start | bytes 4194304
  295.0 22.1 %slice-start.3 = ((s8[6291456]{0:T(1024)(128)(4,1)}), s8[2097152]{0:T(1024)(128)(4,1)S(1)}, s32[]{:S(2)}) async-start(s8[6291456]{0:T(1024)(128)(4,1)} %bitcast.43), calls=%async_computation.6 | async-start | bytes 4194304
  327.7 5.3 copy-start
  327.7 232.6 %all-to-all-start.1 = ((bf16[16,80,4096]{2,1,0:T(8,128)(2,1)}), bf16[16,80,4096]{2,1,0:T(8,128)(2,1)}, u32[]{:S(2)}, u32[]{:S(2)}) async-start(bf16[16,80,4096]{2,1,0:T(8,128)(2,1)} %bitcast.38), calls=%async_computation.1 | async-start | bytes 20971520 | tf_op jit(solution)/shard_map/all_to_all | solution.py:48
Sparse Core Ops, SparseCore 0:
  9.5 38.2 all-gather.1
where the time goes:
time: 577 us; the launch traced here: 576 us
  waiting for transfers between devices  265 us (46%)
  blocking collectives  233 us (40%)
  matrix products  41.9 us (7%)
  between operations  13.5 us (2%)
  local copies, waits for them, and re-layouts  9.33 us (2%)
  other arithmetic  8.6 us (1%)
    all_to_all x1, blocking collectives, on_device(): lax.all_to_all(doubled, 'node', split_axis=0, concat_axis=0, tiled=True)  233 us
    all_to_all x1, waiting for transfers between devices, on_device(): lax.all_to_all(partial_value, 'node', split_axis=0, concat_axis=0, tiled=...  227 us
    all_gather x1, waiting for transfers between devices, on_device(): piece = lax.all_gather(steer_table, 'node', axis=0, tiled=True)  36.9 us
    dot_general x1, matrix products, on_device(): gate = jnp.dot(rows, w_gate[0], preferred_element_type=jnp.float32)  11.8 us
  transfers between devices with their start and end apart: 2, of which 2 were waited for; matrix products, arithmetic and copies ran while one was open for 1% of the time, Pallas kernels for 0%

commit v1 on v0

--- a/solution.py
+++ b/solution.py
@@ -1,10 +1,13 @@
+import functools
 import jax
 import jax.numpy as jnp
 from jax import lax
+from jax.experimental import pallas as pl
+from jax.experimental.pallas import tpu as pltpu
 from jax.sharding import PartitionSpec as P
 
 
-def on_device(
+def on_device_any(
     tokens, steer_table, steer_index, sweep_coef, expert_ids, gate_level, w_gate, w_up, w_down
 ):
     tok_rows, width = tokens.shape
@@ -57,9 +60,308 @@
     return mixed.astype(jnp.bfloat16)
 
 
+CHIPS = 8
+MIB = 1 << 20
+
+
+def node_of(position, core):
+    side = lax.div(position, 4)
+    level = position + side * (7 - 2 * position)
+    return (2 * level + side) * 2 + core
+
+
+def position_of(chip):
+    side, level = lax.rem(chip, 2), lax.div(chip, 2)
+    return level + side * (7 - 2 * level)
+
+
+def ring_kernel(
+    tokens, shard, meta, gate_hbm, up_hbm, down_hbm, out,
+    tok, both, sums, table, metas, steered, act, w_gate, w_up, w_down,
+    w_sem, ag_send, ag_recv, meta_send, meta_recv, tab_send, tab_recv,
+    norm_send, norm_recv, part_send, part_recv, rs_send, rs_recv, free_sem,
+):
+    rows, width = tokens.shape
+    half = rows // 2
+    hidden = w_gate.shape[1]
+    node = lax.axis_index("node")
+    chip, core = lax.div(node, 2), lax.rem(node, 2)
+    here = position_of(chip)
+
+    def ring(distance):
+        return {"node": node_of(lax.rem(here + distance + CHIPS, CHIPS), core)}
+
+    sibling = {"node": 2 * chip + 1 - core}
+    right, left = ring(1), ring(-1)
+    mine = pl.ds(pl.multiple_of(core * rows, rows), rows)
+    others = pl.ds(pl.multiple_of((1 - core) * rows, rows), rows)
+
+    loads = [
+        pltpu.make_async_copy(src, dst, w_sem.at[i])
+        for i, (src, dst) in enumerate(((gate_hbm.at[0], w_gate), (up_hbm.at[0], w_up), (down_hbm.at[0], w_down)))
+    ]
+    for load in loads:
+        load.start()
+
+    barrier = pltpu.get_barrier_semaphore()
+    for distance in range(1, CHIPS):
+        pl.semaphore_signal(barrier, inc=1, device_id=ring(distance), device_id_type=pl.DeviceIdType.MESH)
+    pl.semaphore_signal(barrier, inc=1, device_id=sibling, device_id_type=pl.DeviceIdType.MESH)
+    pl.semaphore_wait(barrier, CHIPS)
+
+    def send(src, dst, send_sem, recv_sem, device):
+        copy = pltpu.make_async_remote_copy(
+            src_ref=src, dst_ref=dst, send_sem=send_sem, recv_sem=recv_sem,
+            device_id=device, device_id_type=pl.DeviceIdType.MESH,
+        )
+        copy.start()
+        return copy
+
+    shard_rows = shard.shape[0]
+    my_shard = pl.ds(pl.multiple_of((core * CHIPS + here) * shard_rows, shard_rows), shard_rows)
+    side_rows = CHIPS * shard_rows
+    my_side = pl.ds(pl.multiple_of(core * side_rows, side_rows), side_rows)
+    meta_copies, tab_copies = {}, {}
+    for distance in range(1, CHIPS):
+        slot = CHIPS - distance
+        tab_copies[slot] = send(shard, table.at[my_shard], tab_send.at[slot], tab_recv.at[slot], ring(distance))
+        meta_copies[slot] = send(meta, metas.at[slot], meta_send.at[slot], meta_recv.at[slot], ring(distance))
+
+    ag = {}
+    ag[1] = send(tokens, tok.at[1], ag_send.at[1], ag_recv.at[1], left)
+    ag[7] = send(tokens, tok.at[7], ag_send.at[7], ag_recv.at[7], right)
+
+    metas[0] = meta[...]
+    table[my_shard, :] = shard[...]
+    sums[3, half:, :] = jnp.zeros((half, width), jnp.bfloat16)
+    sums[5, :half, :] = jnp.zeros((half, width), jnp.bfloat16)
+    for slot in range(1, CHIPS):
+        tab_copies[slot].wait_recv()
+        meta_copies[slot].wait_recv()
+    side_copy = send(table.at[my_side], table.at[my_side], tab_send.at[0], tab_recv.at[0], sibling)
+    side_copy.wait_recv()
+
+    def columns_of(slot):
+        wide = jnp.concatenate([metas[slot], jnp.zeros((128 - meta.shape[0], rows), jnp.float32)], axis=0)
+        return jnp.transpose(wide)
+
+    def pick(columns, which):
+        lanes = lax.broadcasted_iota(jnp.int32, columns.shape, 1)
+        return jnp.sum(jnp.where(lanes == which, columns, 0.0), axis=1, keepdims=True)
+
+    def norm(slot):
+        columns = columns_of(slot)
+        coef, place = pick(columns, CHIPS), pick(columns, CHIPS + 1)
+        lanes = lax.broadcasted_iota(jnp.int32, (rows, table.shape[0]), 1).astype(jnp.float32)
+        tile = 512
+        side_width = table.shape[1]
+        total = jnp.zeros((rows, 1), jnp.float32)
+        for side in range(2):
+            picker = (lanes == place + side).astype(jnp.bfloat16)
+
+            def body(j, total):
+                narrow = pl.ds(pl.multiple_of(j * tile, tile), tile)
+                cols = pl.ds(pl.multiple_of(side * side_width + j * tile, tile), tile)
+                source = tokens[:, cols] if slot == 0 else tok[slot, :, cols]
+                steer = jnp.dot(picker, table[:, narrow], preferred_element_type=jnp.float32)
+                value = source.astype(jnp.float32) + coef * steer
+                steered[:, cols] = value
+                return total + jnp.sum(value * value, axis=1, keepdims=True)
+
+            total = lax.fori_loop(0, side_width // tile, body, total)
+        scale = lax.rsqrt(total * (1.0 / width) + 1e-06)
+
+        @pl.loop(0, width // tile)
+        def _(j):
+            cols = pl.ds(pl.multiple_of(j * tile, tile), tile)
+            both[slot, mine, cols] = (steered[:, cols] * scale).astype(jnp.bfloat16)
+
+        return send(
+            both.at[slot, mine], both.at[slot, mine], norm_send.at[slot], norm_recv.at[slot], sibling
+        )
+
+    def feed_forward(slot):
+        tile = 256
+
+        @pl.loop(0, hidden // tile)
+        def _(j):
+            cols = pl.ds(pl.multiple_of(j * tile, tile), tile)
+            gate = jnp.dot(both[slot], w_gate[:, cols], preferred_element_type=jnp.float32)
+            upper = jnp.dot(both[slot], w_up[:, cols], preferred_element_type=jnp.float32)
+            act[:, cols] = (gate / (1.0 + jnp.exp(-gate)) * upper).astype(jnp.bfloat16)
+
+        tile = 512
+
+        @pl.loop(0, width // tile)
+        def _(j):
+            cols = pl.ds(pl.multiple_of(j * tile, tile), tile)
+            both[slot, :, cols] = jnp.dot(
+                act[...], w_down[:, cols], preferred_element_type=jnp.float32
+            ).astype(jnp.bfloat16)
+
+    def send_partial(slot):
+        return send(both.at[slot, others], tok.at[slot], part_send.at[slot], part_recv.at[slot], sibling)
+
+    def tell_free(slot):
+        pl.semaphore_signal(free_sem.at[slot], inc=1, device_id=sibling, device_id_type=pl.DeviceIdType.MESH)
+
+    norms, parts = {}, {}
+    norms[0] = norm(0)
+    for load in loads:
+        load.wait()
+    norms[0].wait()
+    feed_forward(0)
+    parts[0] = send_partial(0)
+
+    def release(slots):
+        for slot in slots:
+            ag_next[slot].wait_send()
+            tell_free(slot)
+        for slot in slots:
+            pl.semaphore_wait(free_sem.at[slot], 1)
+            parts[slot] = send_partial(slot)
+
+    ag_next = {}
+    for step in (1, 2, 3):
+        up, down = step, CHIPS - step
+        ag[up].wait_recv()
+        if step < 3:
+            ag[up + 1] = ag_next[up] = send(
+                tok.at[up], tok.at[up + 1], ag_send.at[up + 1], ag_recv.at[up + 1], left
+            )
+        else:
+            first = ag_next[up] = send(
+                tok.at[up, pl.ds(0, half)], tok.at[4, pl.ds(0, half)], ag_send.at[4], ag_recv.at[4], left
+            )
+        ag[down].wait_recv()
+        if step < 3:
+            ag[down - 1] = ag_next[down] = send(
+                tok.at[down], tok.at[down - 1], ag_send.at[down - 1], ag_recv.at[down - 1], right
+            )
+        else:
+            second = ag_next[down] = send(
+                tok.at[down, pl.ds(half, half)], tok.at[4, pl.ds(half, half)], ag_send.at[0], ag_recv.at[0], right
+            )
+        for slot in (up, down):
+            norms[slot] = norm(slot)
+        for slot in (up, down):
+            norms[slot].wait()
+            feed_forward(slot)
+        if step > 1:
+            release((step - 1, CHIPS - step + 1))
+    first.wait_recv()
+    second.wait_recv()
+    norms[4] = norm(4)
+    tell_free(4)
+    norms[4].wait()
+    feed_forward(4)
+    pl.semaphore_wait(free_sem.at[4], 1)
+    parts[4] = send_partial(4)
+    release((3, 5))
+
+    def combine(slot, incoming, target):
+        parts[slot].wait_recv()
+        weight = pick(columns_of(slot), chip)
+        tile = 512
+
+        @pl.loop(0, width // tile)
+        def _(j):
+            cols = pl.ds(pl.multiple_of(j * tile, tile), tile)
+            pair = both[slot, mine, cols].astype(jnp.float32) + tok[slot, :, cols].astype(jnp.float32)
+            value = weight * pair.astype(jnp.bfloat16).astype(jnp.float32)
+            for index in incoming:
+                value = value + sums[index, :, cols].astype(jnp.float32)
+            if target is None:
+                both[slot, mine, cols] = value.astype(jnp.bfloat16)
+            else:
+                target[:, cols] = value.astype(jnp.bfloat16)
+
+    combine(4, (), None)
+    low = pl.ds(pl.multiple_of(core * rows, half), half)
+    high = pl.ds(pl.multiple_of(core * rows + half, half), half)
+    rs = {}
+    rs[3] = send(both.at[4, low], sums.at[3, pl.ds(0, half)], rs_send.at[3], rs_recv.at[3], right)
+    rs[5] = send(both.at[4, high], sums.at[5, pl.ds(half, half)], rs_send.at[5], rs_recv.at[5], left)
+    for step in (3, 2, 1):
+        up, down = step, CHIPS - step
+        rs[up].wait_recv()
+        combine(up, (up,), None)
+        after = up - 1
+        rs[after] = send(both.at[up, mine], sums.at[after], rs_send.at[after], rs_recv.at[after], right)
+        rs[down].wait_recv()
+        combine(down, (down,), None)
+        after = down + 1 if down < 7 else 4
+        rs[after] = send(both.at[down, mine], sums.at[after], rs_send.at[after], rs_recv.at[after], left)
+    rs[0].wait_recv()
+    rs[4].wait_recv()
+    combine(0, (0, 4), out)
+
+    for slot in range(CHIPS):
+        rs[slot].wait_send()
+        parts[slot].wait_send()
+    ag[1].wait_send()
+    ag[7].wait_send()
+    side_copy.wait_send()
+    for slot in range(1, CHIPS):
+        tab_copies[slot].wait_send()
+        meta_copies[slot].wait_send()
+
+
+def on_device_ring(
+    tokens, steer_table, steer_index, sweep_coef, expert_ids, gate_level, w_gate, w_up, w_down
+):
+    rows, width = tokens.shape
+    hidden = w_gate.shape[2]
+    per_device = steer_table.shape[0]
+    levels = (gate_level + 1).astype(jnp.float32)
+    share = levels / jnp.sum(levels, axis=1, keepdims=True)
+    hit = expert_ids.T[None, :, :] == lax.iota(jnp.int32, CHIPS)[:, None, None]
+    mixing = jnp.sum(jnp.where(hit, share.T[None, :, :], 0.0), axis=1)
+    owner = steer_index // per_device
+    slot = (owner % 2) * CHIPS + position_of(owner // 2)
+    place = 2 * (slot * per_device + steer_index % per_device)
+    meta = jnp.concatenate(
+        [
+            mixing,
+            sweep_coef[None, :],
+            place.astype(jnp.float32)[None, :],
+            jnp.zeros((16 - CHIPS - 2, rows), jnp.float32),
+        ],
+        axis=0,
+    )
+    shard = steer_table.reshape(2 * per_device, width // 2)
+    vmem = pl.BlockSpec(memory_space=pltpu.VMEM)
+    hbm = pl.BlockSpec(memory_space=pl.ANY)
+    dma = pltpu.SemaphoreType.DMA
+    return pl.pallas_call(
+        ring_kernel,
+        out_shape=jax.ShapeDtypeStruct((rows, width), jnp.bfloat16),
+        in_specs=[vmem, vmem, vmem, hbm, hbm, hbm],
+        out_specs=vmem,
+        scratch_shapes=[
+            pltpu.VMEM((CHIPS, rows, width), jnp.bfloat16),
+            pltpu.VMEM((CHIPS, 2 * rows, width), jnp.bfloat16),
+            pltpu.VMEM((CHIPS, rows, width), jnp.bfloat16),
+            pltpu.VMEM((2 * CHIPS * 2 * per_device, width // 2), jnp.bfloat16),
+            pltpu.VMEM((CHIPS, 16, rows), jnp.float32),
+            pltpu.VMEM((rows, width), jnp.float32),
+            pltpu.VMEM((2 * rows, hidden), jnp.bfloat16),
+            pltpu.VMEM((width, hidden), jnp.bfloat16),
+            pltpu.VMEM((width, hidden), jnp.bfloat16),
+            pltpu.VMEM((hidden, width), jnp.bfloat16),
+            dma((3,)),
+        ]
+        + [dma((CHIPS,)) for _ in range(12)]
+        + [pltpu.SemaphoreType.REGULAR((CHIPS,))],
+        compiler_params=pltpu.CompilerParams(
+            collective_id=0, has_side_effects=True, vmem_limit_bytes=62 * MIB
+        ),
+    )(tokens, shard, meta, w_gate, w_up, w_down)
+
+
 def solution(mesh):
     return jax.shard_map(
-        on_device,
+        on_device_ring if mesh.shape["node"] == 16 else on_device_any,
         mesh=mesh,
         in_specs=(
             P(("groups", "node"), None),

time: 577 us -> 222 us (0.38)
  waiting for transfers between devices: 265 us -> 0 us
  blocking collectives: 233 us -> 0 us
  Pallas kernels: 0 us -> 210 us
  matrix products: 41.9 us -> 0 us
  between operations: 13.5 us -> 0.01 us
    all_to_all x1 -> x0, blocking collectives: 233 us -> none  [on_device(): lax.all_to_all(doubled, 'node', split_axis=0, concat_axis=0, tiled=True)]
    all_to_all x1 -> x0, waiting for transfers between devices: 227 us -> none  [on_device(): lax.all_to_all(partial_value, 'node', split_axis=0, concat_axis=0, tiled=...]
    pallas_call x0 -> x1, Pallas kernels: none -> 210 us  [on_device_ring(): pl.pallas_call(ring_kernel, out_shape=jax.ShapeDtypeStruct((rows, width),...]
    dot_general x7 -> x0, matrix products: 41.9 us -> none  [the longest x1 11.8 us: on_device(): gate = jnp.dot(rows, w_gate[0], preferred_element_type=jnp.float32)]
    all_gather x1 -> x0, waiting for transfers between devices: 36.9 us -> none  [on_device(): piece = lax.all_gather(steer_table, 'node', axis=0, tiled=True)]
    broadcast_in_dim x1, local copies, waits for them, and re-layouts: 7.92 us -> 0.01 us  [on_device_ring(): jnp.zeros((16 - CHIPS - 2, rows), jnp.float32)]
    convert_element_type x2 -> x0, other arithmetic: 6.14 us -> none  [the longest x1 6.13 us: on_device(): total = summed.astype(jnp.bfloat16).reshape(experts * slots, width)]
  transfers between devices with their start and end apart: 2 -> 0, of which waited for: 2 -> 0; matrix products, arithmetic and copies ran while one was open for 1% -> 0% of each run, Pallas kernels for 0% -> 0%
where the time goes in v1:
time: 222 us; the launch traced here: 218 us
  Pallas kernels  210 us (95%)
  other arithmetic  4.08 us (2%)
  local copies, waits for them, and re-layouts  3.86 us (2%)
    pallas_call x1, Pallas kernels, on_device_ring(): pl.pallas_call(ring_kernel, out_shape=jax.ShapeDtypeStruct((rows, width),...  210 us

profile of v1, /device:TPU:13, one launch (start us, length us, event | category | flops | bytes accessed | tf_op | source)
XLA Modules:
  0.0 217.8 jit_solution(14197861715031755141)
XLA Ops:
  0.0 0.7 convert_bitcast_fusion
  0.7 0.7 convert_reduce_fusion
  1.4 0.1 pad.3.clone
  1.5 0.7 divide_bitcast_fusion
  2.2 0.7 select_reduce_fusion
  2.8 1.3 maximum_maximum_fusion.meta
  4.2 1.5 reshape.6.shard
  5.7 209.9 %shard_map.91 = bf16[128,4096]{1,0:T(8,128)(2,1)} custom-call(bf16[128,4096]{1,0:T(8,128)(2,1)} %tokens.1, bf16[16,2048]{1,0:T(8,128)(2,1)} %reshape.6.shard, f32[16,128]{1,0:T(8,128)} %maximum_maximum_fusion.meta, bf16[1,4096,768]{2,1,0:T(8,128)(2,1)} %gate_hbm.1, bf16[1,4096,768]{2,1,0:T(8,128)(2,1)} %up_hbm.1, bf16[1,768,4096]{2,1,0:T(8,128)(2,1)} %down_hbm.1), custom_call_target="tpu_custom_call" | custom-call | tf_op jit(solution)/shard_map/pallas_call | solution.py:336
  215.5 2.3 %copy.11 = bf16[128,4096]{1,0:T(8,128)(2,1)} copy(bf16[128,4096]{1,0:T(8,128)(2,1)} %shard_map.91) | data formatting | bytes 2097152
  (1 shorter events, 0.0 us)

commit v2 on v1

--- a/solution.py
+++ b/solution.py
@@ -61,6 +61,7 @@
 
 
 CHIPS = 8
+PARTS = 2
 MIB = 1 << 20
 
 
@@ -82,7 +83,8 @@
     norm_send, norm_recv, part_send, part_recv, rs_send, rs_recv, free_sem,
 ):
     rows, width = tokens.shape
-    half = rows // 2
+    size = rows // PARTS
+    half = size // 2
     hidden = w_gate.shape[1]
     node = lax.axis_index("node")
     chip, core = lax.div(node, 2), lax.rem(node, 2)
@@ -128,41 +130,55 @@
         meta_copies[slot] = send(meta, metas.at[slot], meta_send.at[slot], meta_recv.at[slot], ring(distance))
 
     ag = {}
-    ag[1] = send(tokens, tok.at[1], ag_send.at[1], ag_recv.at[1], left)
-    ag[7] = send(tokens, tok.at[7], ag_send.at[7], ag_recv.at[7], right)
+    for part in range(PARTS):
+        block = tokens.at[pl.ds(part * size, size)]
+        ag[part, 1] = send(block, tok.at[part, 1], ag_send.at[part, 1], ag_recv.at[part, 1], left)
+        ag[part, 7] = send(block, tok.at[part, 7], ag_send.at[part, 7], ag_recv.at[part, 7], right)
 
     metas[0] = meta[...]
     table[my_shard, :] = shard[...]
-    sums[3, half:, :] = jnp.zeros((half, width), jnp.bfloat16)
-    sums[5, :half, :] = jnp.zeros((half, width), jnp.bfloat16)
+    for part in range(PARTS):
+        sums[part, 3, half:, :] = jnp.zeros((half, width), jnp.bfloat16)
+        sums[part, 5, :half, :] = jnp.zeros((half, width), jnp.bfloat16)
     for slot in range(1, CHIPS):
         tab_copies[slot].wait_recv()
         meta_copies[slot].wait_recv()
     side_copy = send(table.at[my_side], table.at[my_side], tab_send.at[0], tab_recv.at[0], sibling)
     side_copy.wait_recv()
 
-    def columns_of(slot):
+    def columns_of(part, slot):
         wide = jnp.concatenate([metas[slot], jnp.zeros((128 - meta.shape[0], rows), jnp.float32)], axis=0)
-        return jnp.transpose(wide)
+        return jnp.transpose(wide)[part * size:(part + 1) * size]
 
     def pick(columns, which):
         lanes = lax.broadcasted_iota(jnp.int32, columns.shape, 1)
         return jnp.sum(jnp.where(lanes == which, columns, 0.0), axis=1, keepdims=True)
 
-    def norm(slot):
-        columns = columns_of(slot)
+    def place_of(slot):
+        if 1 <= slot <= 4:
+            return slot - 1, 0
+        return (CHIPS - 1 - slot, 1) if slot else (3, 1)
+
+    def rows_of(part, slot, side):
+        group, way = place_of(slot)
+        start = pl.multiple_of(way * 2 * size + side * size, size)
+        return both.at[part, group, pl.ds(start, size)]
+
+    def norm(part, slot):
+        columns = columns_of(part, slot)
         coef, place = pick(columns, CHIPS), pick(columns, CHIPS + 1)
-        lanes = lax.broadcasted_iota(jnp.int32, (rows, table.shape[0]), 1).astype(jnp.float32)
+        lanes = lax.broadcasted_iota(jnp.int32, (size, table.shape[0]), 1).astype(jnp.float32)
         tile = 512
         side_width = table.shape[1]
-        total = jnp.zeros((rows, 1), jnp.float32)
+        total = jnp.zeros((size, 1), jnp.float32)
+        target = rows_of(part, slot, core)
         for side in range(2):
             picker = (lanes == place + side).astype(jnp.bfloat16)
 
             def body(j, total):
                 narrow = pl.ds(pl.multiple_of(j * tile, tile), tile)
                 cols = pl.ds(pl.multiple_of(side * side_width + j * tile, tile), tile)
-                source = tokens[:, cols] if slot == 0 else tok[slot, :, cols]
+                source = tok[part, slot, :, cols] if slot else tokens[pl.ds(part * size, size), cols]
                 steer = jnp.dot(picker, table[:, narrow], preferred_element_type=jnp.float32)
                 value = source.astype(jnp.float32) + coef * steer
                 steered[:, cols] = value
@@ -174,20 +190,20 @@
         @pl.loop(0, width // tile)
         def _(j):
             cols = pl.ds(pl.multiple_of(j * tile, tile), tile)
-            both[slot, mine, cols] = (steered[:, cols] * scale).astype(jnp.bfloat16)
-
-        return send(
-            both.at[slot, mine], both.at[slot, mine], norm_send.at[slot], norm_recv.at[slot], sibling
+            target[:, cols] = (steered[:, cols] * scale).astype(jnp.bfloat16)
+
+        norms[part, slot] = send(
+            target, target, norm_send.at[part, slot], norm_recv.at[part, slot], sibling
         )
 
-    def feed_forward(slot):
+    def feed_forward(part, group):
         tile = 256
 
         @pl.loop(0, hidden // tile)
         def _(j):
             cols = pl.ds(pl.multiple_of(j * tile, tile), tile)
-            gate = jnp.dot(both[slot], w_gate[:, cols], preferred_element_type=jnp.float32)
-            upper = jnp.dot(both[slot], w_up[:, cols], preferred_element_type=jnp.float32)
+            gate = jnp.dot(both[part, group], w_gate[:, cols], preferred_element_type=jnp.float32)
+            upper = jnp.dot(both[part, group], w_up[:, cols], preferred_element_type=jnp.float32)
             act[:, cols] = (gate / (1.0 + jnp.exp(-gate)) * upper).astype(jnp.bfloat16)
 
         tile = 512
@@ -195,112 +211,119 @@
         @pl.loop(0, width // tile)
         def _(j):
             cols = pl.ds(pl.multiple_of(j * tile, tile), tile)
-            both[slot, :, cols] = jnp.dot(
+            both[part, group, :, cols] = jnp.dot(
                 act[...], w_down[:, cols], preferred_element_type=jnp.float32
             ).astype(jnp.bfloat16)
 
-    def send_partial(slot):
-        return send(both.at[slot, others], tok.at[slot], part_send.at[slot], part_recv.at[slot], sibling)
-
-    def tell_free(slot):
-        pl.semaphore_signal(free_sem.at[slot], inc=1, device_id=sibling, device_id_type=pl.DeviceIdType.MESH)
-
-    norms, parts = {}, {}
-    norms[0] = norm(0)
+    def tell_free(part, slot):
+        pl.semaphore_signal(
+            free_sem.at[part, slot], inc=1, device_id=sibling, device_id_type=pl.DeviceIdType.MESH
+        )
+
+    def run_group(part, step):
+        slots = (step, CHIPS - step) if step < 4 else (4, 0)
+        for slot in slots:
+            norms[part, slot].wait()
+        feed_forward(part, step - 1)
+        for slot in slots:
+            if slot % 4:
+                forwards[part, slot].wait_send()
+                tell_free(part, slot)
+        for slot in slots:
+            if slot:
+                pl.semaphore_wait(free_sem.at[part, slot], 1)
+            parts[part, slot] = send(
+                rows_of(part, slot, 1 - core), tok.at[part, slot],
+                part_send.at[part, slot], part_recv.at[part, slot], sibling,
+            )
+
+    norms, parts, forwards = {}, {}, {}
+    for part in range(PARTS):
+        norm(part, 0)
     for load in loads:
         load.wait()
-    norms[0].wait()
-    feed_forward(0)
-    parts[0] = send_partial(0)
-
-    def release(slots):
-        for slot in slots:
-            ag_next[slot].wait_send()
-            tell_free(slot)
-        for slot in slots:
-            pl.semaphore_wait(free_sem.at[slot], 1)
-            parts[slot] = send_partial(slot)
-
-    ag_next = {}
-    for step in (1, 2, 3):
-        up, down = step, CHIPS - step
-        ag[up].wait_recv()
-        if step < 3:
-            ag[up + 1] = ag_next[up] = send(
-                tok.at[up], tok.at[up + 1], ag_send.at[up + 1], ag_recv.at[up + 1], left
-            )
-        else:
-            first = ag_next[up] = send(
-                tok.at[up, pl.ds(0, half)], tok.at[4, pl.ds(0, half)], ag_send.at[4], ag_recv.at[4], left
-            )
-        ag[down].wait_recv()
-        if step < 3:
-            ag[down - 1] = ag_next[down] = send(
-                tok.at[down], tok.at[down - 1], ag_send.at[down - 1], ag_recv.at[down - 1], right
-            )
-        else:
-            second = ag_next[down] = send(
-                tok.at[down, pl.ds(half, half)], tok.at[4, pl.ds(half, half)], ag_send.at[0], ag_recv.at[0], right
-            )
-        for slot in (up, down):
-            norms[slot] = norm(slot)
-        for slot in (up, down):
-            norms[slot].wait()
-            feed_forward(slot)
-        if step > 1:
-            release((step - 1, CHIPS - step + 1))
-    first.wait_recv()
-    second.wait_recv()
-    norms[4] = norm(4)
-    tell_free(4)
-    norms[4].wait()
-    feed_forward(4)
-    pl.semaphore_wait(free_sem.at[4], 1)
-    parts[4] = send_partial(4)
-    release((3, 5))
-
-    def combine(slot, incoming, target):
-        parts[slot].wait_recv()
-        weight = pick(columns_of(slot), chip)
+    waiting = None
+    for step in (1, 2, 3, 4):
+        for part in range(PARTS):
+            if step < 4:
+                for slot, after, device in ((step, step + 1, left), (CHIPS - step, CHIPS - step - 1, right)):
+                    ag[part, slot].wait_recv()
+                    if step < 3:
+                        src, dst, index = tok.at[part, slot], tok.at[part, after], after
+                    else:
+                        piece = pl.ds(0 if device is left else half, half)
+                        src, dst = tok.at[part, slot, piece], tok.at[part, 4, piece]
+                        index = 4 if device is left else 0
+                    forwards[part, slot] = send(
+                        src, dst, ag_send.at[part, index], ag_recv.at[part, index], device
+                    )
+                    ag[part, index] = forwards[part, slot]
+                norm(part, step)
+                norm(part, CHIPS - step)
+            else:
+                ag[part, 4].wait_recv()
+                ag[part, 0].wait_recv()
+                norm(part, 4)
+                tell_free(part, 4)
+            if waiting is not None:
+                run_group(*waiting)
+            waiting = (part, step)
+
+    def combine(part, slot, incoming, target):
+        parts[part, slot].wait_recv()
+        weight = pick(columns_of(part, slot), chip)
+        own = rows_of(part, slot, core)
         tile = 512
 
         @pl.loop(0, width // tile)
         def _(j):
             cols = pl.ds(pl.multiple_of(j * tile, tile), tile)
-            pair = both[slot, mine, cols].astype(jnp.float32) + tok[slot, :, cols].astype(jnp.float32)
+            pair = own[:, cols].astype(jnp.float32) + tok[part, slot, :, cols].astype(jnp.float32)
             value = weight * pair.astype(jnp.bfloat16).astype(jnp.float32)
             for index in incoming:
-                value = value + sums[index, :, cols].astype(jnp.float32)
-            if target is None:
-                both[slot, mine, cols] = value.astype(jnp.bfloat16)
-            else:
-                target[:, cols] = value.astype(jnp.bfloat16)
-
-    combine(4, (), None)
-    low = pl.ds(pl.multiple_of(core * rows, half), half)
-    high = pl.ds(pl.multiple_of(core * rows + half, half), half)
+                value = value + sums[part, index, :, cols].astype(jnp.float32)
+            target[:, cols] = value.astype(jnp.bfloat16)
+
     rs = {}
-    rs[3] = send(both.at[4, low], sums.at[3, pl.ds(0, half)], rs_send.at[3], rs_recv.at[3], right)
-    rs[5] = send(both.at[4, high], sums.at[5, pl.ds(half, half)], rs_send.at[5], rs_recv.at[5], left)
+
+    def far_sums(part):
+        combine(part, 4, (), rows_of(part, 4, core))
+        start = pl.multiple_of(core * size, size)
+        low = both.at[part, 3, pl.ds(start, half)]
+        high = both.at[part, 3, pl.ds(pl.multiple_of(start + half, half), half)]
+        rs[part, 3] = send(
+            low, sums.at[part, 3, pl.ds(0, half)], rs_send.at[part, 3], rs_recv.at[part, 3], right
+        )
+        rs[part, 5] = send(
+            high, sums.at[part, 5, pl.ds(half, half)], rs_send.at[part, 5], rs_recv.at[part, 5], left
+        )
+
+    for part in range(PARTS - 1):
+        far_sums(part)
+    run_group(*waiting)
+    far_sums(PARTS - 1)
     for step in (3, 2, 1):
-        up, down = step, CHIPS - step
-        rs[up].wait_recv()
-        combine(up, (up,), None)
-        after = up - 1
-        rs[after] = send(both.at[up, mine], sums.at[after], rs_send.at[after], rs_recv.at[after], right)
-        rs[down].wait_recv()
-        combine(down, (down,), None)
-        after = down + 1 if down < 7 else 4
-        rs[after] = send(both.at[down, mine], sums.at[after], rs_send.at[after], rs_recv.at[after], left)
-    rs[0].wait_recv()
-    rs[4].wait_recv()
-    combine(0, (0, 4), out)
-
-    for slot in range(CHIPS):
-        rs[slot].wait_send()
-        parts[slot].wait_send()
-    ag[1].wait_send()
-    ag[7].wait_send()
+        for part in range(PARTS):
+            for slot, after, device in (
+                (step, step - 1, right), (CHIPS - step, CHIPS - step + 1 if step > 1 else 4, left)
+            ):
+                rs[part, slot].wait_recv()
+                own = rows_of(part, slot, core)
+                combine(part, slot, (slot,), own)
+                rs[part, after] = send(
+                    own, sums.at[part, after], rs_send.at[part, after], rs_recv.at[part, after], device
+                )
+    for part in range(PARTS):
+        rs[part, 0].wait_recv()
+        rs[part, 4].wait_recv()
+        combine(part, 0, (0, 4), out.at[pl.ds(part * size, size)])
+
+    for part in range(PARTS):
+        for slot in range(CHIPS):
+            rs[part, slot].wait_send()
+            parts[part, slot].wait_send()
+        ag[part, 1].wait_send()
+        ag[part, 7].wait_send()
     side_copy.wait_send()
     for slot in range(1, CHIPS):
         tab_copies[slot].wait_send()
@@ -339,20 +362,22 @@
         in_specs=[vmem, vmem, vmem, hbm, hbm, hbm],
         out_specs=vmem,
         scratch_shapes=[
-            pltpu.VMEM((CHIPS, rows, width), jnp.bfloat16),
-            pltpu.VMEM((CHIPS, 2 * rows, width), jnp.bfloat16),
-            pltpu.VMEM((CHIPS, rows, width), jnp.bfloat16),
+            pltpu.VMEM((PARTS, CHIPS, rows // PARTS, width), jnp.bfloat16),
+            pltpu.VMEM((PARTS, CHIPS // 2, 4 * rows // PARTS, width), jnp.bfloat16),
+            pltpu.VMEM((PARTS, CHIPS, rows // PARTS, width), jnp.bfloat16),
             pltpu.VMEM((2 * CHIPS * 2 * per_device, width // 2), jnp.bfloat16),
             pltpu.VMEM((CHIPS, 16, rows), jnp.float32),
-            pltpu.VMEM((rows, width), jnp.float32),
+            pltpu.VMEM((rows // PARTS, width), jnp.float32),
             pltpu.VMEM((2 * rows, hidden), jnp.bfloat16),
             pltpu.VMEM((width, hidden), jnp.bfloat16),
             pltpu.VMEM((width, hidden), jnp.bfloat16),
             pltpu.VMEM((hidden, width), jnp.bfloat16),
             dma((3,)),
         ]
-        + [dma((CHIPS,)) for _ in range(12)]
-        + [pltpu.SemaphoreType.REGULAR((CHIPS,))],
+        + [dma((PARTS, CHIPS)), dma((PARTS, CHIPS))]
+        + [dma((CHIPS,)) for _ in range(4)]
+        + [dma((PARTS, CHIPS)) for _ in range(6)]
+        + [pltpu.SemaphoreType.REGULAR((PARTS, CHIPS))],
         compiler_params=pltpu.CompilerParams(
             collective_id=0, has_side_effects=True, vmem_limit_bytes=62 * MIB
         ),

time: 222 us -> 219 us (0.986)
  no operation moved by 1% of the time
where the time goes in v2:
time: 219 us; the launch traced here: 216 us
  Pallas kernels  208 us (95%)
  other arithmetic  4.08 us (2%)
  local copies, waits for them, and re-layouts  3.86 us (2%)
    pallas_call x1, Pallas kernels, on_device_ring(): pl.pallas_call(ring_kernel, out_shape=jax.ShapeDtypeStruct((rows, width),...  208 us

profile of v2, /device:TPU:13, one launch (start us, length us, event | category | flops | bytes accessed | tf_op | source)
XLA Modules:
  0.0 215.8 jit_solution(12160448559482612964)
XLA Ops:
  0.0 0.7 convert_bitcast_fusion
  0.7 0.7 convert_reduce_fusion
  1.4 0.1 pad.3.clone
  1.5 0.7 divide_bitcast_fusion
  2.2 0.7 select_reduce_fusion
  2.8 1.3 maximum_maximum_fusion.meta
  4.2 1.5 reshape.6.shard
  5.7 207.9 %shard_map.91 = bf16[128,4096]{1,0:T(8,128)(2,1)} custom-call(bf16[128,4096]{1,0:T(8,128)(2,1)} %tokens.1, bf16[16,2048]{1,0:T(8,128)(2,1)} %reshape.6.shard, f32[16,128]{1,0:T(8,128)} %maximum_maximum_fusion.meta, bf16[1,4096,768]{2,1,0:T(8,128)(2,1)} %gate_hbm.1, bf16[1,4096,768]{2,1,0:T(8,128)(2,1)} %up_hbm.1, bf16[1,768,4096]{2,1,0:T(8,128)(2,1)} %down_hbm.1), custom_call_target="tpu_custom_call" | custom-call | tf_op jit(solution)/shard_map/pallas_call | solution.py:359
  213.5 2.3 %copy.11 = bf16[128,4096]{1,0:T(8,128)(2,1)} copy(bf16[128,4096]{1,0:T(8,128)(2,1)} %shard_map.91) | data formatting | bytes 2097152
  (1 shorter events, 0.0 us)
